TPU v7x, 128 devices: a whole 4x4x4 slice. The times are simulated.
128 devices in a mesh: blk: 32 (over y_lo, x, z), fsdp: 4 (over y_hi, core).
Axes of the slice: x: 4, y: 4 (y_hi: 2, y_lo: 2; y = y_hi * 2 + y_lo), z: 4, core: 2. Of those that a mesh axis runs over, the one named last changes fastest.
Arguments:
- tokens: bfloat16 [2, 8192, 1024], P(None, ('blk', 'fsdp')), may hold values from -6 to 6
- cotangent: bfloat16 [2, 8192, 1024], P(None, ('blk', 'fsdp')), may hold values from -6 to 6
- w_attn: float32 [4, 1024, 1024], P(None, ('blk', 'fsdp')), as said below
- w_ffn_in: float32 [2, 1024, 2816], P(None, ('blk', 'fsdp')), may hold values from -0.1875 to 0.1875
- w_down: float32 [2816, 1024], P(('blk', 'fsdp')), may hold values from -0.109375 to 0.109375
- gains: float32 [2, 1024], P(None, ('blk', 'fsdp')), may hold values from 0.5 to 1.5
- m_attn: float32 [4, 1024, 1024], P(None, ('blk', 'fsdp')), as said below
- m_ffn_in: float32 [2, 1024, 2816], P(None, ('blk', 'fsdp')), as said below
- m_down: float32 [2816, 1024], P(('blk', 'fsdp')), as said below
- m_gains: float32 [2, 1024], P(None, ('blk', 'fsdp')), as said below
- v_attn: float32 [4, 1024, 1024], P(None, ('blk', 'fsdp')), as said below
- v_ffn_in: float32 [2, 1024, 2816], P(None, ('blk', 'fsdp')), as said below
- v_down: float32 [2816, 1024], P(('blk', 'fsdp')), as said below
- v_gains: float32 [2, 1024], P(None, ('blk', 'fsdp')), as said below
Outputs:
- output: bfloat16 [2, 8192, 1024], P(None, ('blk', 'fsdp'))
- grad_inputs: float32 [2, 8192, 1024], P(None, ('blk', 'fsdp'))
- grad_attn: float32 [4, 1024, 1024], P(None, ('blk', 'fsdp'))
- grad_ffn_in: float32 [2, 1024, 2816], P(None, ('blk', 'fsdp'))
- grad_down: float32 [2816, 1024], P(('blk', 'fsdp'))
- grad_gains: float32 [2, 1024], P(None, ('blk', 'fsdp'))
- new_attn: float32 [4, 1024, 1024], P(None, ('blk', 'fsdp'))
- new_ffn_in: float32 [2, 1024, 2816], P(None, ('blk', 'fsdp'))
- new_down: float32 [2816, 1024], P(('blk', 'fsdp'))
- new_gains: float32 [2, 1024], P(None, ('blk', 'fsdp'))
- second_attn: float32 [4, 1024, 1024], P(None, ('blk', 'fsdp'))
- second_ffn_in: float32 [2, 1024, 2816], P(None, ('blk', 'fsdp'))
- second_down: float32 [2816, 1024], P(('blk', 'fsdp'))
- second_gains: float32 [2, 1024], P(None, ('blk', 'fsdp'))
Inputs may be any that keep to these rules, and one draw needn't show every extreme that they name: `w_attn`: independent entries. `m_attn`: independent entries of both signs. `m_ffn_in`: independent entries of both signs. `m_down`: independent entries of both signs. `m_gains`: independent entries of both signs. `v_attn`: positive entries. `v_ffn_in`: positive entries. `v_down`: positive entries. `v_gains`: positive entries.
All inputs are finite; a program needn't handle non-finite values.
Results may differ from a plain program's by a relative error of at most 0.017.
The roundings to bfloat16 on the way count: a program that leaves them out, or rounds other values in their place, can miss the bound.
Values may be sent and summed in bfloat16 or wider, within the bound.
A program may use at most 384 MiB of HBM per device.

v0:
```python
import math

import jax
import jax.numpy as jnp
from jax import lax
from jax.sharding import PartitionSpec as P

HEADS = 16
HEAD = 64
STEP = 10


EPSILON = 1e-05
BETA_ONE = 0.9
BETA_TWO = 0.999
ADAM_EPS = 1e-08


def normalize(values):
    inverse = lax.rsqrt(jnp.mean(values * values, axis=-1, keepdims=True) + EPSILON)
    return (values * inverse, inverse)


def norm_back(grad_hat, scaled, inverse):
    return inverse * (grad_hat - scaled * jnp.mean(grad_hat * scaled, axis=-1, keepdims=True))


def outer_sum(left, right):
    return lax.dot_general(
        left, right, (((0,), (0,)), ((), ())), preferred_element_type=jnp.float32
    )


def times_back(grad, weight):
    return lax.dot_general(
        grad, weight, (((1,), (1,)), ((), ())), preferred_element_type=jnp.float32
    )


def by_heads(values):
    return values.reshape(values.shape[0], values.shape[1], HEADS, HEAD)


def block_loop(span_rows, advance, running):
    blk_rows = math.gcd(span_rows, 512)
    return lax.fori_loop(
        0,
        span_rows // blk_rows,
        lambda turn_idx, carried: advance(turn_idx * blk_rows, blk_rows, carried),
        running,
    )


def forward_fold(queries, query_pos, length_bias, score_scale):
    final_pos = query_pos[-1]

    def forward_accumulate(running, shards, first_row):
        key_rows, value_rows = shards

        def advance(offset, blk_rows, carried):
            key_blk = by_heads(lax.dynamic_slice_in_dim(key_rows, offset, blk_rows, 1))
            val_blk = by_heads(lax.dynamic_slice_in_dim(value_rows, offset, blk_rows, 1))
            key_pos = offset + jnp.arange(blk_rows, dtype=jnp.int32)
            logits = (
                jnp.einsum("sqhd,skhd->shqk", queries, key_blk, preferred_element_type=jnp.float32)
                * score_scale
                - length_bias
            )
            visible = (query_pos[:, None] >= key_pos[None, :])[None, None]
            weights = jnp.where(visible, jax.nn.sigmoid(logits), 0.0).astype(jnp.bfloat16)
            return carried + jnp.einsum(
                "shqk,skhd->sqhd", weights, val_blk, preferred_element_type=jnp.float32
            )

        return lax.cond(
            first_row <= final_pos,
            lambda carried: block_loop(key_rows.shape[1], advance, carried),
            lambda carried: carried,
            running,
        )

    return forward_accumulate


def query_grad_fold(queries, grad_out, query_pos, length_bias, score_scale):
    final_pos = query_pos[-1]

    def query_accumulate(running, shards, first_row):
        key_rows, value_rows = shards

        def advance(offset, blk_rows, carried):
            key_blk = by_heads(lax.dynamic_slice_in_dim(key_rows, offset, blk_rows, 1))
            val_blk = by_heads(lax.dynamic_slice_in_dim(value_rows, offset, blk_rows, 1))
            key_pos = offset + jnp.arange(blk_rows, dtype=jnp.int32)
            logits = (
                jnp.einsum("sqhd,skhd->shqk", queries, key_blk, preferred_element_type=jnp.float32)
                * score_scale
                - length_bias
            )
            visible = (query_pos[:, None] >= key_pos[None, :])[None, None]
            squashed = jax.nn.sigmoid(logits)
            prob_grad = jnp.einsum(
                "sqhd,skhd->shqk", grad_out, val_blk, preferred_element_type=jnp.float32
            )
            score_grad = jnp.where(visible, prob_grad * (squashed * (1.0 - squashed)), 0.0).astype(
                jnp.bfloat16
            )
            return (
                carried
                + jnp.einsum(
                    "shqk,skhd->sqhd", score_grad, key_blk, preferred_element_type=jnp.float32
                )
                * score_scale
            )

        return lax.cond(
            first_row <= final_pos,
            lambda carried: block_loop(key_rows.shape[1], advance, carried),
            lambda carried: carried,
            running,
        )

    return query_accumulate


def key_grad_fold(key_rows, value_rows, key_pos, length_bias, score_scale):
    lowest_pos = key_pos[0]

    def key_accumulate(running, shards, first_row):
        query_rows, grad_rows = shards
        span_rows = query_rows.shape[1]

        def advance(offset, blk_rows, carried):
            key_acc, value_acc = carried
            query_blk = by_heads(lax.dynamic_slice_in_dim(query_rows, offset, blk_rows, 1))
            grad_blk = by_heads(lax.dynamic_slice_in_dim(grad_rows, offset, blk_rows, 1))
            query_pos = offset + jnp.arange(blk_rows, dtype=jnp.int32)
            logits = (
                jnp.einsum(
                    "sqhd,skhd->shqk", query_blk, key_rows, preferred_element_type=jnp.float32
                )
                * score_scale
                - length_bias
            )
            visible = (query_pos[:, None] >= key_pos[None, :])[None, None]
            squashed = jax.nn.sigmoid(logits)
            weights = jnp.where(visible, squashed, 0.0).astype(jnp.bfloat16)
            value_acc = value_acc + jnp.einsum(
                "shqk,sqhd->skhd", weights, grad_blk, preferred_element_type=jnp.float32
            )
            prob_grad = jnp.einsum(
                "sqhd,skhd->shqk", grad_blk, value_rows, preferred_element_type=jnp.float32
            )
            score_grad = jnp.where(visible, prob_grad * (squashed * (1.0 - squashed)), 0.0).astype(
                jnp.bfloat16
            )
            key_acc = (
                key_acc
                + jnp.einsum(
                    "shqk,sqhd->skhd", score_grad, query_blk, preferred_element_type=jnp.float32
                )
                * score_scale
            )
            return (key_acc, value_acc)

        return lax.cond(
            first_row + span_rows - 1 >= lowest_pos,
            lambda carried: block_loop(span_rows, advance, carried),
            lambda carried: carried,
            running,
        )

    return key_accumulate


def adam_step(weight, first, second, grad, rate, decay):
    first_new = BETA_ONE * first + (1.0 - BETA_ONE) * grad
    second_new = BETA_TWO * second + (1.0 - BETA_TWO) * grad * grad
    direction = (
        first_new
        / (1.0 - BETA_ONE**STEP)
        / (jnp.sqrt(second_new / (1.0 - BETA_TWO**STEP)) + ADAM_EPS)
    )
    return (weight - rate * (direction + decay * weight), second_new)


def body(
    tokens,
    cotangent,
    w_attn,
    w_ffn_in,
    w_down,
    gains,
    m_attn,
    m_ffn_in,
    m_down,
    m_gains,
    v_attn,
    v_ffn_in,
    v_down,
    v_gains,
):
    seqs_here, rows_here, width = tokens.shape
    total_rows = seqs_here * rows_here
    length_bias = math.log(rows_here * lax.axis_size(("blk", "fsdp")))
    score_scale = HEAD ** (-0.5)
    own_pos = lax.axis_index(("blk", "fsdp")) * rows_here + jnp.arange(rows_here, dtype=jnp.int32)
    attn_full, gains_full = (
        lax.all_gather(w_attn.astype(jnp.bfloat16), ("blk", "fsdp"), axis=1, tiled=True),
        lax.all_gather(gains.astype(jnp.bfloat16), ("blk", "fsdp"), axis=1, tiled=True),
    )
    ffn_full, down_full = (
        lax.all_gather(w_ffn_in.astype(jnp.bfloat16), ("blk", "fsdp"), axis=1, tiled=True),
        lax.all_gather(w_down.astype(jnp.bfloat16), ("blk", "fsdp"), axis=0, tiled=True),
    )
    gain_one = gains_full[0].astype(jnp.float32)
    gain_two = gains_full[1].astype(jnp.float32)
    inputs = tokens.astype(jnp.float32).reshape(total_rows, width)
    scaled_one, inverse_one = normalize(inputs)
    normed_one = (scaled_one * gain_one).astype(jnp.bfloat16)
    queries = (
        jnp.dot(normed_one, attn_full[0], preferred_element_type=jnp.float32)
        .astype(jnp.bfloat16)
        .reshape(seqs_here, rows_here, width)
    )
    key_rows = (
        jnp.dot(normed_one, attn_full[1], preferred_element_type=jnp.float32)
        .astype(jnp.bfloat16)
        .reshape(seqs_here, rows_here, width)
    )
    value_rows = (
        jnp.dot(normed_one, attn_full[2], preferred_element_type=jnp.float32)
        .astype(jnp.bfloat16)
        .reshape(seqs_here, rows_here, width)
    )
    empty = jnp.zeros((seqs_here, rows_here, HEADS, HEAD), jnp.float32)
    fold_forward = forward_fold(by_heads(queries), own_pos, length_bias, score_scale)
    attended = fold_forward(
        empty,
        (
            lax.all_gather(key_rows, ("blk", "fsdp"), axis=1, tiled=True),
            lax.all_gather(value_rows, ("blk", "fsdp"), axis=1, tiled=True),
        ),
        jnp.int32(0),
    )
    attn_out = attended.reshape(total_rows, width).astype(jnp.bfloat16)
    middle = inputs + jnp.dot(attn_out, attn_full[3], preferred_element_type=jnp.float32)
    scaled_two, inverse_two = normalize(middle)
    normed_two = (scaled_two * gain_two).astype(jnp.bfloat16)
    gate = jnp.dot(normed_two, ffn_full[0], preferred_element_type=jnp.float32)
    upward = jnp.dot(normed_two, ffn_full[1], preferred_element_type=jnp.float32)
    hidden = (jax.nn.silu(gate) * upward).astype(jnp.bfloat16)
    result = middle + jnp.dot(hidden, down_full, preferred_element_type=jnp.float32)
    output = result.astype(jnp.bfloat16).reshape(seqs_here, rows_here, width)
    grad_rows = cotangent.reshape(total_rows, width)
    grad_dn = outer_sum(hidden, grad_rows)
    grad_hidden = times_back(grad_rows, down_full)
    squash = jax.nn.sigmoid(gate)
    grad_up = (grad_hidden * jax.nn.silu(gate)).astype(jnp.bfloat16)
    grad_gate = (grad_hidden * upward * (squash + gate * squash * (1.0 - squash))).astype(
        jnp.bfloat16
    )
    ffn_grad = jnp.stack([outer_sum(normed_two, grad_gate), outer_sum(normed_two, grad_up)])
    ffn_part, down_part = (
        lax.psum_scatter(ffn_grad, ("blk", "fsdp"), scatter_dimension=1, tiled=True),
        lax.psum_scatter(grad_dn, ("blk", "fsdp"), scatter_dimension=0, tiled=True),
    )
    grad_normed_two = times_back(grad_gate, ffn_full[0]) + times_back(grad_up, ffn_full[1])
    gain_grad_two = jnp.sum(grad_normed_two * scaled_two, axis=0)
    grad_middle = grad_rows.astype(jnp.float32) + norm_back(
        grad_normed_two * gain_two, scaled_two, inverse_two
    )
    branch_grad = grad_middle.astype(jnp.bfloat16)
    grad_out_proj = outer_sum(attn_out, branch_grad)
    grad_attended = (
        times_back(branch_grad, attn_full[3])
        .astype(jnp.bfloat16)
        .reshape(seqs_here, rows_here, width)
    )
    fold_queries = query_grad_fold(
        by_heads(queries), by_heads(grad_attended), own_pos, length_bias, score_scale
    )
    grad_queries = fold_queries(
        empty,
        (
            lax.all_gather(key_rows, ("blk", "fsdp"), axis=1, tiled=True),
            lax.all_gather(value_rows, ("blk", "fsdp"), axis=1, tiled=True),
        ),
        jnp.int32(0),
    )
    fold_keys = key_grad_fold(
        by_heads(key_rows), by_heads(value_rows), own_pos, length_bias, score_scale
    )
    grad_keys, grad_values = fold_keys(
        (empty, empty),
        (
            lax.all_gather(queries, ("blk", "fsdp"), axis=1, tiled=True),
            lax.all_gather(grad_attended, ("blk", "fsdp"), axis=1, tiled=True),
        ),
        jnp.int32(0),
    )
    grad_q_rows = grad_queries.reshape(total_rows, width).astype(jnp.bfloat16)
    grad_k_rows = grad_keys.reshape(total_rows, width).astype(jnp.bfloat16)
    grad_v_rows = grad_values.reshape(total_rows, width).astype(jnp.bfloat16)
    attn_grad = jnp.stack(
        [
            outer_sum(normed_one, grad_q_rows),
            outer_sum(normed_one, grad_k_rows),
            outer_sum(normed_one, grad_v_rows),
            grad_out_proj,
        ]
    )
    grad_normed_one = (
        times_back(grad_q_rows, attn_full[0])
        + times_back(grad_k_rows, attn_full[1])
        + times_back(grad_v_rows, attn_full[2])
    )
    gain_grad_one = jnp.sum(grad_normed_one * scaled_one, axis=0)
    gain_grad = jnp.stack([gain_grad_one, gain_grad_two])
    attn_part, gain_part = (
        lax.psum_scatter(attn_grad, ("blk", "fsdp"), scatter_dimension=1, tiled=True),
        lax.psum_scatter(gain_grad, ("blk", "fsdp"), scatter_dimension=1, tiled=True),
    )
    grad_inputs = grad_middle + norm_back(grad_normed_one * gain_one, scaled_one, inverse_one)
    new_attn, second_attn = adam_step(w_attn, m_attn, v_attn, attn_part, 0.06, 0.1)
    new_ffn, second_ffn = adam_step(w_ffn_in, m_ffn_in, v_ffn_in, ffn_part, 0.06, 0.1)
    new_dn, second_dn = adam_step(w_down, m_down, v_down, down_part, 0.04, 0.1)
    new_gn, second_gn = adam_step(gains, m_gains, v_gains, gain_part, 0.4, 0.0)
    return (
        output,
        grad_inputs.reshape(seqs_here, rows_here, width),
        attn_part,
        ffn_part,
        down_part,
        gain_part,
        new_attn,
        new_ffn,
        new_dn,
        new_gn,
        second_attn,
        second_ffn,
        second_dn,
        second_gn,
    )


def solution(mesh):
    placed = (
        P(None, ("blk", "fsdp"), None),
        P(None, ("blk", "fsdp"), None),
        P(None, ("blk", "fsdp"), None),
        P(None, ("blk", "fsdp"), None),
        P(("blk", "fsdp"), None),
        P(None, ("blk", "fsdp")),
        P(None, ("blk", "fsdp"), None),
        P(None, ("blk", "fsdp"), None),
        P(("blk", "fsdp"), None),
        P(None, ("blk", "fsdp")),
        P(None, ("blk", "fsdp"), None),
        P(None, ("blk", "fsdp"), None),
        P(("blk", "fsdp"), None),
        P(None, ("blk", "fsdp")),
    )
    return jax.shard_map(
        body,
        mesh=mesh,
        in_specs=placed,
        out_specs=(
            P(None, ("blk", "fsdp"), None),
            P(None, ("blk", "fsdp"), None),
            P(None, ("blk", "fsdp"), None),
            P(None, ("blk", "fsdp"), None),
            P(("blk", "fsdp"), None),
            P(None, ("blk", "fsdp")),
            P(None, ("blk", "fsdp"), None),
            P(None, ("blk", "fsdp"), None),
            P(("blk", "fsdp"), None),
            P(None, ("blk", "fsdp")),
            P(None, ("blk", "fsdp"), None),
            P(None, ("blk", "fsdp"), None),
            P(("blk", "fsdp"), None),
            P(None, ("blk", "fsdp")),
        ),
        check_vma=False,
    )
```

profile of v0, /device:TPU:1, one launch (start us, length us, event | category | flops | bytes accessed | tf_op | source)
XLA Modules:
  0.0 2946.7 jit_solution(12150226569443483237)
XLA Ops:
  11.1 179.3 %all-gather = bf16[128,8,2]{1,2,0:T(2,128)(2,1)S(1)} all-gather(bf16[1,8,2]{1,2,0:T(2,128)(2,1)S(1)} %convert_bitcast_fusion.1), channel_id=1, replica_groups=mesh['blk'=32,'fsdp'=4] {'blk','fsdp'}, dimensions={0}, use_global_device_ids=true | all-gather | bytes 4128 | tf_op jit(solution)/shard_map/all_gather | solution.py:210
  193.3 23.0 all-gather.10.cloned.1.call-done
  229.0 189.5 %all-gather.22.cloned.1.call-done = bf16[128,22,1024]{2,1,0:T(8,128)(2,1)} async-done(((bf16[1,22,1024]{2,1,0:T(8,128)(2,1)}), bf16[128,22,1024]{2,1,0:T(8,128)(2,1)}) %all-gather.22.cloned.1.call-update) | async-done | bytes 5767184 | tf_op jit(solution)/shard_map/all_gather | solution.py:214
  418.5 9.4 reshape.354
  428.2 228.5 %all-gather.12.cloned.1.call-done = bf16[2,8192,1024]{2,0,1:T(2,128)(2,1)} async-done(((bf16[2,64,1024]{2,0,1:T(2,128)(2,1)}), bf16[2,8192,1024]{2,0,1:T(2,128)(2,1)}) %all-gather.12.cloned.1.call-update) | async-done | bytes 33554448 | tf_op jit(solution)/shard_map/all_gather | solution.py:242
  656.7 237.9 %all-gather.14.cloned.1.call-done = bf16[2,8192,1024]{2,0,1:T(2,128)(2,1)} async-done(((bf16[2,64,1024]{2,0,1:T(2,128)(2,1)}), bf16[2,8192,1024]{2,0,1:T(2,128)(2,1)}) %all-gather.14.cloned.1.call-update) | async-done | bytes 33554448 | tf_op jit(solution)/shard_map/all_gather | solution.py:241
  894.6 363.4 %conditional.3 = (f32[2,64,16,64]{1,3,2,0:T(8,128)}) conditional(s32[]{:T(128)} %bitcast.1, () %tuple.100, (bf16[2,8192,1024]{2,0,1:T(2,128)(2,1)}, s32[64]{0:T(128)S(1)}, bf16[2,8192,1024]{2,0,1:T(2,128)(2,1)}, bf16[2,64,16,64]{3,2,1,0:T(8,128)(2,1)S(1)}) %tuple.101), branch_computations={%region_1.0_spmd, %region_2.5_spmd} | conditional | flops 276070912 | bytes 22876684 | solution.py:75
  894.8 362.8 %while.47 = (s32[]{:T(128)}, f32[2,64,16,64]{1,3,2,0:T(8,128)}, bf16[2,8192,1024]{2,0,1:T(2,128)(2,1)}, s32[64]{0:T(128)S(1)}, bf16[2,8192,1024]{2,0,1:T(2,128)(...) while((s32[]{:T(128)}, f32[2,64,16,64]{1,3,2,0:T(8,128)}, ...), condition=%wide.region_4.4_spmd.clone, body=%wide.region_3.3_spmd.clone.sunk | while | flops 276070912 | bytes 22352300 | solution.py:46
  917.3 6.5 constant_dynamic-slice_fusion.15
  939.9 6.5 constant_dynamic-slice_fusion.15
  962.5 6.5 constant_dynamic-slice_fusion.15
  1007.9 6.5 constant_dynamic-slice_fusion.15
  1030.5 6.5 constant_dynamic-slice_fusion.15
  1121.0 6.5 constant_dynamic-slice_fusion.15
  1143.8 6.5 constant_dynamic-slice_fusion.15
  1166.5 6.5 constant_dynamic-slice_fusion.15
  1189.3 6.5 constant_dynamic-slice_fusion.15
  1212.1 6.5 constant_dynamic-slice_fusion.15
  1234.9 6.5 constant_dynamic-slice_fusion.15
  1287.0 8.2 pad_maximum_fusion
  1295.9 440.5 %conditional.4 = (bf16[128,1024]{1,0:T(8,128)(2,1)S(1)}) conditional(s32[]{:T(128)} %bitcast.1, () %tuple.102, (bf16[128,1024]{1,0:T(8,128)(2,1)S(1)}, bf16[2,8192,1024]{2,0,1:T(2,128)(2,1)}, s32[64]{0:T(128)S(1)}, bf16[2,8192,1024]{2,0,1:T(2,128)(2,1)}, bf16[2,64,16,64]{3,2,1,0:T(8,128)(2,1)S(1)}) %tuple.103), branch_computations={%region_7.8_spmd, %region_8.0_spmd} | conditional | flops 413696512 | bytes 37556792 | solution.py:116
  1299.4 434.9 %while.48 = (s32[]{:T(128)}, f32[2,64,16,64]{1,3,2,0:T(8,128)}, bf16[2,8192,1024]{2,0,1:T(2,128)(2,1)}, s32[64]{0:T(128)S(1)}, bf16[2,8192,1024]{2,0,1:T(2,128)(...) while((s32[]{:T(128)}, f32[2,64,16,64]{1,3,2,0:T(8,128)}, ...), condition=%wide.region_10.10_spmd.clone, body=%wide.region_9.9_spmd.clone.sunk | while | flops 413565440 | bytes 33100212 | solution.py:46
  1299.5 7.1 constant_dynamic-slice_fusion.14
  1326.3 7.1 constant_dynamic-slice_fusion.14
  1353.3 7.2 constant_dynamic-slice_fusion.14
  1380.6 7.2 constant_dynamic-slice_fusion.14
  1408.0 7.3 constant_dynamic-slice_fusion.14
  1435.3 7.3 constant_dynamic-slice_fusion.14
  1462.7 7.2 constant_dynamic-slice_fusion.14
  1490.0 7.3 constant_dynamic-slice_fusion.14
  1517.5 7.2 constant_dynamic-slice_fusion.14
  1544.6 7.1 constant_dynamic-slice_fusion.14
  1571.7 7.1 constant_dynamic-slice_fusion.14
  1598.8 7.1 constant_dynamic-slice_fusion.14
  1625.9 7.2 constant_dynamic-slice_fusion.14
  1653.0 7.1 constant_dynamic-slice_fusion.14
  1680.2 7.1 constant_dynamic-slice_fusion.14
  1707.3 7.1 constant_dynamic-slice_fusion.14
  1742.0 485.1 %conditional.5 = (bf16[128,1024]{1,0:T(8,128)(2,1)}, bf16[128,1024]{1,0:T(8,128)(2,1)}) conditional(s32[]{:T(128)} %bitcast.19, () %tuple.104, (bf16[128,1024]{1,0:T(8,128)(2,1)S(1)}, bf16[128,1024]{1,0:T(8,128)(2,1)S(1)}, bf16[2,8192,1024]{2,0,1:T(2,128)(2,1)}, s32[64]{0:T(128)S(1)}, bf16[2,8192,1024]{2,0,1:T(2,128)(2,1)}) %tuple.214), branch_computations={%region_11.12_spmd, %region_12.15_spmd} | conditional | flops 549356032 | bytes 46240308 | solution.py:166
  1744.8 477.7 %while.49 = (s32[]{:T(128)}, f32[2,64,16,64]{1,3,2,0:T(8,128)}, f32[2,64,16,64]{1,3,2,0:T(8,128)S(1)}, bf16[2,8192,1024]{2,0,1:T(2,128)(2,1)}, s32[64]{0:T(128)S...) while((s32[]{:T(128)}, f32[2,64,16,64]{1,3,2,0:T(8,128)}, ...), condition=%wide.region_14.14_spmd.clone, body=%wide.region_13.13_spmd.clone.sunk | while | flops 549093888 | bytes 40473020 | solution.py:46
  1864.1 6.5 constant_dynamic-slice_fusion.13
  1894.0 6.5 constant_dynamic-slice_fusion.13
  2103.0 6.5 constant_dynamic-slice_fusion.13
  2244.6 383.6 %fusion = f32[24,1024]{1,0:T(8,128)S(1)} fusion(f32[2816,1024]{1,0:T(8,128)} %fusion.65), kind=kCustom, calls=%all-reduce-scatter | all-reduce-scatter fusion | flops 3145729 | bytes 11632640
  2636.2 8.4 collective-permute-start.4
  2644.6 6.6 collective-permute-start.3
  2683.4 82.6 %all-reduce.1 = f32[2,1024]{1,0:T(2,128)S(1)} all-reduce(f32[2,1024]{1,0:T(2,128)S(1)} %pad_maximum_fusion.2), channel_id=5, replica_groups=mesh['blk'=32,'fsdp'=4] {'blk','fsdp'}, use_global_device_ids=true, to_apply=%region_21.22.clone | all-reduce | flops 2048 | bytes 16384
  2767.6 170.3 %reduce-scatter.6.cloned.1.call-done = f32[4,8,1024]{2,1,0:T(8,128)} async-done(((f32[4,1024,1024]{2,1,0:T(8,128)}), f32[4,8,1024]{2,1,0:T(8,128)}) %reduce-scatter.6.cloned.1.call-update) | async-done | bytes 131088 | tf_op jit(solution)/shard_map/reduce_scatter | solution.py:321
  (523 shorter events, 1194.8 us)
Async XLA Ops:
  7.2 209.2 %all-gather.10.cloned.1.call-start = ((), (), s32[]{:S(2)}) async-start(), calls=%async_computation.2 | async-start | bytes 8454144 | tf_op jit(solution)/shard_map/all_gather | solution.py:209
  8.8 409.7 %all-gather.22.cloned.1.call-start = ((), (), s32[]{:S(2)}) async-start(), calls=%async_computation.10 | async-start | bytes 6340608 | tf_op jit(solution)/shard_map/all_gather | solution.py:214
  10.4 646.3 %all-gather.12.cloned.1.call-start = ((), (), s32[]{:S(2)}) async-start(), calls=%async_computation.3 | async-start | bytes 33816576 | tf_op jit(solution)/shard_map/all_gather | solution.py:242
  191.6 32.3 %copy-start.22 = (f32[2,8,2816]{2,1,0:T(8,128)S(1)}, f32[2,8,2816]{2,1,0:T(8,128)}, u32[]{:S(2)}) copy-start(f32[2,8,2816]{2,1,0:T(8,128)} %param.29) | copy-start | bytes 540676
  191.6 33.0 %copy-start.37 = (f32[2,64]{1,0:T(2,128)}, f32[2,64]{1,0:T(2,128)S(1)}, u32[]{:S(2)}) copy-start(f32[2,64]{1,0:T(2,128)S(1)} %add_rsqrt_fusion) | copy-start | bytes 1540
  193.3 33.4 %copy-start.7 = (bf16[2,64,1024]{2,1,0:T(8,128)(2,1)}, bf16[2,64,1024]{2,1,0:T(8,128)(2,1)S(1)}, u32[]{:S(2)}) copy-start(bf16[2,64,1024]{2,1,0:T(8,128)(2,1)S(1)} %multiply_convert_fusion.4) | copy-start | bytes 786436
  220.1 674.5 %all-gather.14.cloned.1.call-start = ((), (), s32[]{:S(2)}) async-start(), calls=%async_computation.4 | async-start | bytes 33816576 | tf_op jit(solution)/shard_map/all_gather | solution.py:241
  223.9 1038.7 %all-gather.16.cloned.1.call-start = ((), (), s32[]{:S(2)}) async-start(), calls=%async_computation.5 | async-start | bytes 11624448 | tf_op jit(solution)/shard_map/all_gather | solution.py:213
  224.6 1517.3 %all-gather.18.cloned.1.call-start = ((), (), s32[]{:S(2)}) async-start(), calls=%async_computation.6 | async-start | bytes 33816576 | tf_op jit(solution)/shard_map/all_gather | solution.py:297
  227.7 1514.2 %all-gather.20.cloned.1.call-start = ((), (), s32[]{:S(2)}) async-start(), calls=%async_computation.7 | async-start | bytes 33816576 | tf_op jit(solution)/shard_map/all_gather | solution.py:298
  894.6 365.5 %copy-start.9 = (bf16[2,64,1024]{2,1,0:T(8,128)(2,1)S(1)}, bf16[2,64,1024]{2,1,0:T(8,128)(2,1)}, u32[]{:S(2)}) copy-start(bf16[2,64,1024]{2,1,0:T(8,128)(2,1)} %param.26) | copy-start | bytes 786436
  1260.1 6.3 copy-start.16
  1262.4 16.1 copy-start.4
  1262.6 8.1 slice-start
  1262.6 11.3 slice-start.2
  1266.4 7.5 slice-start.3
  1278.7 460.5 %copy-start.2 = (f32[128,1024]{1,0:T(8,128)}, f32[128,1024]{1,0:T(8,128)S(1)}, u32[]{:S(2)}) copy-start(f32[128,1024]{1,0:T(8,128)S(1)} %multiply_add_fusion.1) | copy-start | bytes 1572868
  1282.4 1391.3 %reduce-scatter.8.cloned.1.call-start = ((), (), s32[]{:S(2)}) async-start(), calls=%async_computation.9 | async-start | bytes 23248896 | tf_op jit(solution)/shard_map/reduce_scatter | solution.py:265
  1295.2 1642.8 %reduce-scatter.6.cloned.1.call-start = ((), (), s32[]{:S(2)}) async-start(), calls=%async_computation.8 | async-start | bytes 16908288 | tf_op jit(solution)/shard_map/reduce_scatter | solution.py:321
  1295.9 440.5 %copy-start.8 = (bf16[2,64,1024]{2,1,0:T(8,128)(2,1)S(1)}, bf16[2,64,1024]{2,1,0:T(8,128)(2,1)}, u32[]{:S(2)}) copy-start(bf16[2,64,1024]{2,1,0:T(8,128)(2,1)} %copy-done.7) | copy-start | bytes 786436
  1736.4 5.6 copy-start.12
  2244.6 391.5 %copy-start.38 = (f32[2,64]{1,0:T(2,128)S(1)}, f32[2,64]{1,0:T(2,128)}, u32[]{:S(2)}) copy-start(f32[2,64]{1,0:T(2,128)} %copy-done.37) | copy-start | bytes 1540
  2244.6 416.0 %copy-start.5 = (f32[128,1024]{1,0:T(8,128)S(1)}, f32[128,1024]{1,0:T(8,128)}, u32[]{:S(2)}) copy-start(f32[128,1024]{1,0:T(8,128)} %copy-done.4) | copy-start | bytes 1572868
  2628.2 6.5 collective-permute-start.10
  2629.5 6.7 collective-permute-start.9
  2630.8 13.8 collective-permute-start.8
  2632.1 19.1 collective-permute-start.7
  2633.4 19.1 collective-permute-start.6
  2634.8 20.9 collective-permute-start.5
  2636.2 35.8 %copy-start.26 = (f32[22,1024]{1,0:T(8,128)S(1)}, f32[22,1024]{1,0:T(8,128)}, u32[]{:S(2)}) copy-start(f32[22,1024]{1,0:T(8,128)} %param.30) | copy-start | bytes 270340
  2636.2 37.5 %copy-start.23 = (f32[2,8,2816]{2,1,0:T(8,128)S(1)}, f32[2,8,2816]{2,1,0:T(8,128)}, u32[]{:S(2)}) copy-start(f32[2,8,2816]{2,1,0:T(8,128)} %param.29) | copy-start | bytes 540676
  2636.2 37.5 %copy-start.27 = (f32[2,8,2816]{2,1,0:T(8,128)S(1)}, f32[2,8,2816]{2,1,0:T(8,128)}, u32[]{:S(2)}) copy-start(f32[2,8,2816]{2,1,0:T(8,128)} %param.33) | copy-start | bytes 540676
  2636.2 37.5 %copy-start.28 = (f32[2,8,2816]{2,1,0:T(8,128)S(1)}, f32[2,8,2816]{2,1,0:T(8,128)}, u32[]{:S(2)}) copy-start(f32[2,8,2816]{2,1,0:T(8,128)} %param.37) | copy-start | bytes 540676
  2636.2 28.6 collective-permute-start.4
  2644.6 20.2 collective-permute-start.3
  2651.3 13.6 collective-permute-start.2
  2652.6 12.3 collective-permute-start.1
  2655.7 10.5 collective-permute-start
  2672.0 8.8 copy-start.10
  2672.0 8.8 copy-start.13
  2672.0 8.8 copy-start.35
  2678.1 87.9 %copy-start.40 = (f32[2,8]{1,0:T(2,128)S(1)}, f32[2,8]{1,0:T(2,128)}, u32[]{:S(2)}) copy-start(f32[2,8]{1,0:T(2,128)} %param.31) | copy-start | bytes 196
  2678.1 87.9 %copy-start.41 = (f32[2,8]{1,0:T(2,128)S(1)}, f32[2,8]{1,0:T(2,128)}, u32[]{:S(2)}) copy-start(f32[2,8]{1,0:T(2,128)} %param.35) | copy-start | bytes 196
  2678.1 87.9 %copy-start.42 = (f32[2,8]{1,0:T(2,128)S(1)}, f32[2,8]{1,0:T(2,128)}, u32[]{:S(2)}) copy-start(f32[2,8]{1,0:T(2,128)} %param.39) | copy-start | bytes 196
  2678.1 88.5 %copy-start.3 = (f32[128,1024]{1,0:T(8,128)S(1)}, f32[128,1024]{1,0:T(8,128)}, u32[]{:S(2)}) copy-start(f32[128,1024]{1,0:T(8,128)} %copy-done.2) | copy-start | bytes 1572868
  2678.1 259.9 %copy-start.25 = (f32[4,8,1024]{2,1,0:T(8,128)S(1)}, f32[4,8,1024]{2,1,0:T(8,128)}, u32[]{:S(2)}) copy-start(f32[4,8,1024]{2,1,0:T(8,128)} %param.28) | copy-start | bytes 393220
  2678.1 259.9 %copy-start.29 = (f32[4,8,1024]{2,1,0:T(8,128)S(1)}, f32[4,8,1024]{2,1,0:T(8,128)}, u32[]{:S(2)}) copy-start(f32[4,8,1024]{2,1,0:T(8,128)} %param.32) | copy-start | bytes 393220
  2678.1 259.9 %copy-start.30 = (f32[4,8,1024]{2,1,0:T(8,128)S(1)}, f32[4,8,1024]{2,1,0:T(8,128)}, u32[]{:S(2)}) copy-start(f32[4,8,1024]{2,1,0:T(8,128)} %param.36) | copy-start | bytes 393220
  (20 other events, 49.9 us)
Sparse Core Ops, SparseCore 0:
  10.3 205.9 all-gather.9
  218.6 199.8 all-gather.21
  420.8 235.8 all-gather.11
  658.9 235.6 all-gather.13
  896.7 206.0 all-gather.15
  1104.4 235.8 all-gather.17
  1342.6 235.7 all-gather.19
  1581.4 674.6 reduce-scatter.7
  2259.1 678.8 reduce-scatter.5
where the time goes:
time: 2970 us; the launch traced here: 2950 us
  local copies, waits for them, and re-layouts  853 us (29%)
  waiting for transfers between devices  849 us (29%)
  blocking collectives  645 us (22%)
  matrix products  511 us (17%)
  other arithmetic  36.5 us (1%)
  starting transfers between devices  32.4 us (1%)
    unnamed x2, blocking collectives  466 us
    dynamic_slice x48, local copies, waits for them, and re-layouts, advance(): lax.dynamic_slice_in_dim(value_rows, offset, blk_rows, 1)  313 us
    dynamic_slice x48, local copies, waits for them, and re-layouts, advance(): key_blk = by_heads(lax.dynamic_slice_in_dim(key_rows, offset, blk_rows, 1))  253 us
    all_gather x1, waiting for transfers between devices, body(): lax.all_gather(key_rows, ('blk', 'fsdp'), axis=1, tiled=True)  238 us
    all_gather x1, waiting for transfers between devices, body(): lax.all_gather(value_rows, ('blk', 'fsdp'), axis=1, tiled=True)  229 us
    all_gather x1, waiting for transfers between devices, body(): lax.all_gather(w_down.astype(jnp.bfloat16), ('blk', 'fsdp'), axis=0, tile...  189 us
    all_gather x1, blocking collectives, body(): lax.all_gather(gains.astype(jnp.bfloat16), ('blk', 'fsdp'), axis=1, tiled...  179 us
    dynamic_slice x32, local copies, waits for them, and re-layouts, advance(): lax.dynamic_slice_in_dim(grad_rows, offset, blk_rows, 1)  178 us
  transfers between devices with their start and end apart: 20, of which 5 were waited for; matrix products, arithmetic and copies ran while one was open for 60% of the time, Pallas kernels for 0%

commit v1 on v0

v1 whole, which is shorter than its diff:
```python
import math

import jax
import jax.numpy as jnp
from jax import lax
from jax.experimental import pallas as pl
from jax.experimental.pallas import tpu as pltpu
from jax.sharding import Mesh
from jax.sharding import PartitionSpec as P

HEADS = 16
HEAD = 64
WIDTH = 1024
FF = 2816
HALF = FF // 2
STEP = 10
EPSILON = 1e-05
BETA_ONE = 0.9
BETA_TWO = 0.999
ADAM_EPS = 1e-08
F32 = jnp.float32
BF16 = jnp.bfloat16
AXES = ("yl", "x", "z", "yh", "core")
SWAP = [(0, 1), (1, 0)]
MESH_ID = pl.DeviceIdType.MESH
ORDERS = (("x", "y", "z"), ("y", "z", "x"), ("z", "x", "y"))
PERIODS = 8
TILE = 256
LOG2E = 1.4426950408889634


def coords():
    place = {a: lax.axis_index(a) for a in AXES}
    place["y"] = place["yh"] * 2 + place["yl"]
    return place


def step_id(place, axis, off):
    v = lax.rem(place[axis] + off, 4)
    if axis == "y":
        return {"yl": lax.rem(v, 2), "yh": v // 2}
    return {axis: v}


def region(place, done, axis, v):
    def pick(a):
        return slice(None) if a in done else (v if a == axis else place[a])

    y = pick("y")
    if isinstance(y, slice):
        return (y, pick("x"), pick("z"), y)
    return (lax.rem(y, 2), pick("x"), pick("z"), y // 2)


def halves(cols):
    lo, hi = cols
    mid = lo + ((hi - lo) // 128 + 1) // 2 * 128
    return (lo, mid), (mid, hi)


def split3(width):
    tiles = width // 128
    a = (tiles + 2) // 3
    b = (tiles - a + 1) // 2
    return [(0, a * 128), (a * 128, (a + b) * 128), ((a + b) * 128, width)]


def ring_barrier(place):
    bar = pltpu.get_barrier_semaphore()
    for axis in ("x", "y", "z"):
        for off in (1, 3):
            pl.semaphore_signal(
                bar, inc=1, device_id=step_id(place, axis, off), device_id_type=MESH_ID
            )
    pl.semaphore_wait(bar, 6)


def remote(src, dst, ssem, rsem, i, dev):
    return pltpu.make_async_remote_copy(
        src_ref=src,
        dst_ref=dst,
        send_sem=ssem.at[i],
        recv_sem=rsem.at[i],
        device_id=dev,
        device_id_type=MESH_ID,
    )


def gather_kernel(shard, out, lsem, ssem, rsem):
    place = coords()
    ring_barrier(place)
    parts = split3(shard.shape[-1])
    own = out.at[place["yl"], place["x"], place["z"], place["yh"]]
    local = pltpu.make_async_copy(shard, own, lsem)
    local.start()

    def at(idx, cols):
        return out.at[idx + (slice(None), slice(cols[0], cols[1]))]

    sends = []
    for k in range(3):
        if k == 1:
            local.wait()
        todo = [
            (order[k], order[:k], cols, (k * 3 + p) * 4)
            for p, (order, cols) in enumerate(zip(ORDERS, parts))
        ]
        for axis, done, cols, base in todo:
            me = region(place, done, axis, place[axis])
            src = shard.at[:, cols[0] : cols[1]] if k == 0 else at(me, cols)
            for j, off in enumerate((1, 3)):
                d = remote(src, at(me, cols), ssem, rsem, base + j, step_id(place, axis, off))
                d.start()
                sends.append(d)
        for axis, done, cols, base in todo:
            for j, (off, half) in enumerate(zip((3, 1), halves(cols))):
                got = region(place, done, axis, lax.rem(place[axis] + off, 4))
                r = at(got, cols)
                remote(r, r, ssem, rsem, base + j, step_id(place, axis, off)).wait_recv()
                r = at(got, half)
                d = remote(r, r, ssem, rsem, base + 2 + j, step_id(place, axis, 4 - off))
                d.start()
                sends.append(d)
        for axis, done, cols, base in todo:
            far = region(place, done, axis, lax.rem(place[axis] + 2, 4))
            for j, half in enumerate(halves(cols)):
                r = at(far, half)
                remote(r, r, ssem, rsem, base + 2 + j, step_id(place, axis, 1)).wait_recv()
    for d in sends:
        d.wait_send()


def gather_chips(shard, cid, name):
    return pl.pallas_call(
        gather_kernel,
        out_shape=jax.ShapeDtypeStruct((2, 4, 4, 2) + shard.shape, shard.dtype),
        in_specs=[pl.BlockSpec(memory_space=pl.ANY)],
        out_specs=pl.BlockSpec(memory_space=pl.ANY),
        scratch_shapes=[
            pltpu.SemaphoreType.DMA,
            pltpu.SemaphoreType.DMA((36,)),
            pltpu.SemaphoreType.DMA((36,)),
        ],
        compiler_params=pltpu.CompilerParams(collective_id=cid, has_side_effects=True),
        name=name,
    )(shard).reshape(64 * shard.shape[0], shard.shape[1])


def lead(place, done, axis, v):
    return region(place, done, axis, v)


def scatter_kernel(grads, out, *rest):
    place = coords()
    parts = split3(grads.shape[-1])
    work = rest[0:3]
    bufs = rest[3:12]
    lsem, ssem, rsem = rest[12:]
    loads = []
    for p, cols in enumerate(parts):
        d = pltpu.make_async_copy(
            grads.at[:, :, :, :, :, cols[0] : cols[1]], work[p], lsem.at[p]
        )
        d.start()
        loads.append(d)
    ring_barrier(place)
    sends = []
    for k in range(3):
        todo = []
        for p, (order, cols) in enumerate(zip(ORDERS, parts)):
            back = order[::-1]
            axis, left = back[k], back[k + 1 :]
            todo.append((p, axis, left, halves((0, cols[1] - cols[0])), (k * 3 + p) * 4))
        if k == 0:
            for d in loads:
                d.wait()

        def dims(left):
            return tuple(
                n
                for n, a in zip((2, 4, 4, 2), ("y", "x", "z", "y"))
                if a in left
            )

        def chunk(p, left, axis, off, cols):
            idx = region(place, left, axis, lax.rem(place[axis] + off, 4))
            return work[p].at[idx + (slice(None), slice(cols[0], cols[1]))]

        def buf(p, k, j, cols):
            b = bufs[p * 3 + k]
            return b.at[(j,) + (slice(None),) * (len(b.shape) - 2) + (slice(cols[0], cols[1]),)]

        for p, axis, left, hv, base in todo:
            for j, off in enumerate((1, 3)):
                d = remote(
                    chunk(p, left, axis, 2, hv[j]),
                    buf(p, k, j, hv[j]),
                    ssem,
                    rsem,
                    base + j,
                    step_id(place, axis, off),
                )
                d.start()
                sends.append(d)
        for p, axis, left, hv, base in todo:
            whole = (0, hv[1][1])
            for j, off in enumerate((1, 3)):
                r = buf(p, k, j, hv[j])
                remote(r, r, ssem, rsem, base + j, step_id(place, axis, 4 - off)).wait_recv()
                add_into(chunk(p, left, axis, off, hv[j]), [r])
                d = remote(
                    chunk(p, left, axis, off, whole),
                    buf(p, k, j + 2, whole),
                    ssem,
                    rsem,
                    base + 2 + j,
                    step_id(place, axis, off),
                )
                d.start()
                sends.append(d)
        for p, axis, left, hv, base in todo:
            whole = (0, hv[1][1])
            got = []
            for j, off in enumerate((1, 3)):
                r = buf(p, k, j + 2, whole)
                remote(r, r, ssem, rsem, base + 2 + j, step_id(place, axis, 4 - off)).wait_recv()
                got.append(r)
            if k < 2:
                add_into(chunk(p, left, axis, 0, whole), got)
            else:
                total = chunk(p, left, axis, 0, whole)[...].astype(F32)
                for r in got:
                    total = total + r[...].astype(F32)
                out[:, parts[p][0] : parts[p][1]] = total
    for d in sends:
        d.wait_send()


def add_into(target, terms):
    dims = target.shape[:-2]
    count = math.prod(dims)

    def one(i, _):
        idx = []
        for n in reversed(dims):
            idx.append(lax.rem(i, n))
            i = i // n
        idx = tuple(reversed(idx))
        total = target[idx].astype(F32)
        for t in terms:
            total = total + t[idx].astype(F32)
        target[idx] = total.astype(BF16)
        return 0

    lax.fori_loop(0, count, one, 0)


def scatter_chips(grads, cid, name):
    width = grads.shape[-1]
    parts = split3(width)
    size = {"y": (2, 2), "x": (4,), "z": (4,)}
    scratch = [pltpu.VMEM((2, 4, 4, 2, 16, hi - lo), BF16) for lo, hi in parts]
    for order, (lo, hi) in zip(ORDERS, parts):
        back = order[::-1]
        for k in range(3):
            left = back[k + 1 :]
            dims = tuple(
                n for n, a in zip((2, 4, 4, 2), ("y", "x", "z", "y")) if a in left
            )
            scratch.append(pltpu.VMEM((4,) + dims + (16, hi - lo), BF16))
    scratch += [
        pltpu.SemaphoreType.DMA((3,)),
        pltpu.SemaphoreType.DMA((36,)),
        pltpu.SemaphoreType.DMA((36,)),
    ]
    return pl.pallas_call(
        scatter_kernel,
        out_shape=jax.ShapeDtypeStruct((16, width), F32),
        in_specs=[pl.BlockSpec(memory_space=pl.ANY)],
        out_specs=pl.BlockSpec(memory_space=pltpu.VMEM),
        scratch_shapes=scratch,
        compiler_params=pltpu.CompilerParams(
            collective_id=cid, has_side_effects=True, vmem_limit_bytes=56 * 1024 * 1024
        ),
        name=name,
    )(grads.reshape(2, 4, 4, 2, 16, width))


def dot_nt(a, b):
    return lax.dot_general(a, b, (((1,), (1,)), ((), ())), preferred_element_type=F32)


def dot_nn(a, b):
    return lax.dot_general(a, b, (((1,), (0,)), ((), ())), preferred_element_type=F32)


def sigmoid_of(raw):
    return 1.0 / (1.0 + jnp.exp2(raw * (-LOG2E / 8.0) + 13.0))


def z_barrier(place):
    bar = pltpu.get_barrier_semaphore()
    for off in (1, 2, 3):
        pl.semaphore_signal(bar, inc=1, device_id=step_id(place, "z", off), device_id_type=MESH_ID)
    pl.semaphore_wait(bar, 3)


def attend_kernel(qkv, kv_all, att, acc, ssem, rsem):
    place = coords()
    z = place["z"]
    z_barrier(place)

    def rows(p):
        return pl.ds(pl.multiple_of(p * TILE, TILE), TILE)

    def piece(p, j, off):
        return remote(
            qkv.at[rows(p), 128:256],
            kv_all.at[z, rows(p)],
            ssem,
            rsem,
            p * 3 + j,
            step_id(place, "z", off),
        )

    def start(p, _):
        for j, off in enumerate((1, 3, 2)):
            piece(p, j, off).start()
        return 0

    lax.fori_loop(0, PERIODS, start, 0)
    kv_all[z] = qkv[:, 128:256]

    def tile(p, _):
        for j, off in enumerate((3, 1, 2)):
            r = kv_all.at[lax.rem(z + off, 4), rows(p)]
            remote(r, r, ssem, rsem, p * 3 + j, step_id(place, "z", off)).wait_recv()
        q = qkv[rows(p), 0:128]
        acc[...] = jnp.zeros_like(acc)

        def earlier(r, _):
            total = acc[...]
            for zz in range(4):
                kv = kv_all[zz, rows(r)]
                total = total + dot_nn(sigmoid_of(dot_nt(q, kv)).astype(BF16), kv)
            acc[...] = total
            return 0

        lax.fori_loop(0, p, earlier, 0)
        total = acc[...]
        q_pos = z * TILE + lax.broadcasted_iota(jnp.int32, (TILE, TILE), 0)
        k_pos = lax.broadcasted_iota(jnp.int32, (TILE, TILE), 1)
        for zz in range(4):
            kv = kv_all[zz, rows(p)]
            w = jnp.where(q_pos >= k_pos + zz * TILE, sigmoid_of(dot_nt(q, kv)), 0.0)
            total = total + dot_nn(w.astype(BF16), kv)
        att[rows(p), :] = total.astype(BF16)
        return 0

    lax.fori_loop(0, PERIODS, tile, 0)

    def end(p, _):
        for j, off in enumerate((1, 3, 2)):
            piece(p, j, off).wait_send()
        return 0

    lax.fori_loop(0, PERIODS, end, 0)


def attend(qkv, cid):
    n = qkv.shape[0]
    return pl.pallas_call(
        attend_kernel,
        out_shape=(
            jax.ShapeDtypeStruct((4, n, 128), BF16),
            jax.ShapeDtypeStruct((n, 128), BF16),
        ),
        in_specs=[pl.BlockSpec(memory_space=pltpu.VMEM)],
        out_specs=[pl.BlockSpec(memory_space=pltpu.VMEM)] * 2,
        scratch_shapes=[
            pltpu.VMEM((TILE, 128), F32),
            pltpu.SemaphoreType.DMA((24,)),
            pltpu.SemaphoreType.DMA((24,)),
        ],
        compiler_params=pltpu.CompilerParams(
            collective_id=cid, has_side_effects=True, vmem_limit_bytes=48 * 1024 * 1024
        ),
        name="attend",
    )(qkv)


def attend_back_kernel(qkv, kv_all, da_all, out, kvt, acc, dqt, own, stage, got, ssem, rsem):
    place = coords()
    z = place["z"]
    z_barrier(place)
    dqt[...] = jnp.zeros_like(dqt)

    def rows(p):
        return pl.ds(pl.multiple_of(p * TILE, TILE), TILE)

    def piece(r, j, off):
        return remote(
            stage.at[lax.rem(z + off, 4), rows(r)],
            got.at[j, rows(r)],
            ssem,
            rsem,
            r * 3 + j,
            step_id(place, "z", off),
        )

    def keys(r, _):
        for zz in range(4):
            kvt[zz] = jnp.transpose(kv_all[zz, rows(r)].astype(F32)).astype(BF16)
        acc[...] = jnp.zeros_like(acc)

        def block(p, masked):
            q = qkv[rows(p), 0:128]
            da = da_all[rows(p), :]
            dq = dqt[:, rows(p)]
            if masked:
                q_pos = z * TILE + lax.broadcasted_iota(jnp.int32, (TILE, TILE), 1)
                k_pos = lax.broadcasted_iota(jnp.int32, (TILE, TILE), 0)
            for zz in range(4):
                kv = kv_all[zz, rows(r)]
                sg = sigmoid_of(dot_nt(kv, q))
                if masked:
                    sg = jnp.where(q_pos >= k_pos + zz * TILE, sg, 0.0)
                ds = (dot_nt(kv, da) * (sg * (1.0 - sg))).astype(BF16)
                acc[zz] += dot_nn(ds, q) + dot_nn(sg.astype(BF16), da)
                dq = dq + dot_nn(kvt[zz], ds)
            dqt[:, rows(p)] = dq

        block(r, True)

        def later(p, _):
            block(p, False)
            return 0

        lax.fori_loop(r + 1, PERIODS, later, 0)
        for zz in range(4):
            stage[zz, rows(r)] = acc[zz].astype(BF16)
        own[rows(r), :] = acc[z]
        for j, off in enumerate((1, 3, 2)):
            piece(r, j, off).start()
        return 0

    lax.fori_loop(0, PERIODS, keys, 0)
    scale = jnp.where(lax.broadcasted_iota(jnp.int32, (TILE, 128), 1) < HEAD, 0.125, 1.0)

    def finish(p, _):
        total = own[rows(p), :]
        for j, off in enumerate((1, 3, 2)):
            piece(p, j, off).wait()
            total = total + got[j, rows(p)].astype(F32)
        out[rows(p), 128:256] = (total * scale).astype(BF16)
        out[rows(p), 0:128] = (jnp.transpose(dqt[:, rows(p)]) * 0.125).astype(BF16)
        return 0

    lax.fori_loop(0, PERIODS, finish, 0)


def attend_back(qkv, kv_all, da, cid):
    n = qkv.shape[0]
    return pl.pallas_call(
        attend_back_kernel,
        out_shape=jax.ShapeDtypeStruct((n, 256), BF16),
        in_specs=[pl.BlockSpec(memory_space=pltpu.VMEM)] * 3,
        out_specs=pl.BlockSpec(memory_space=pltpu.VMEM),
        scratch_shapes=[
            pltpu.VMEM((4, 128, TILE), BF16),
            pltpu.VMEM((4, TILE, 128), F32),
            pltpu.VMEM((128, n), F32),
            pltpu.VMEM((n, 128), F32),
            pltpu.VMEM((4, n, 128), BF16),
            pltpu.VMEM((3, n, 128), BF16),
            pltpu.SemaphoreType.DMA((24,)),
            pltpu.SemaphoreType.DMA((24,)),
        ],
        compiler_params=pltpu.CompilerParams(
            collective_id=cid, has_side_effects=True, vmem_limit_bytes=48 * 1024 * 1024
        ),
        name="attend_back",
    )(qkv, kv_all, da)


def normalize(values):
    inverse = lax.rsqrt(jnp.mean(values * values, axis=-1, keepdims=True) + EPSILON)
    return (values * inverse, inverse)


def norm_back(grad_hat, scaled, inverse):
    return inverse * (grad_hat - scaled * jnp.mean(grad_hat * scaled, axis=-1, keepdims=True))


def outer_sum(left, right):
    return lax.dot_general(left, right, (((0,), (0,)), ((), ())), preferred_element_type=F32)


def adam_step(weight, first, second, grad, rate, decay):
    first_new = BETA_ONE * first + (1.0 - BETA_ONE) * grad
    second_new = BETA_TWO * second + (1.0 - BETA_TWO) * grad * grad
    direction = (
        first_new
        / (1.0 - BETA_ONE**STEP)
        / (jnp.sqrt(second_new / (1.0 - BETA_TWO**STEP)) + ADAM_EPS)
    )
    return (weight - rate * (direction + decay * weight), second_new)


def other_core(values):
    return lax.ppermute(values, "core", SWAP)


def both(core, values, axis):
    other = other_core(values)
    first = jnp.where(core == 0, values, other)
    last = jnp.where(core == 0, other, values)
    return jnp.concatenate([first, last], axis=axis)


def by_core(values):
    cut = values.reshape(values.shape[0], 64, 2, 22)
    main = jnp.moveaxis(cut[..., :16], 2, 0).reshape(2, values.shape[0], 1024)
    tail = jnp.moveaxis(cut[..., 16:], 2, 0).reshape(2, values.shape[0], 384)
    return jnp.concatenate([main, tail], axis=-1)


def from_cores(values):
    n = values.shape[1]
    main = jnp.moveaxis(values[..., :1024].reshape(2, n, 64, 16), 0, 2)
    tail = jnp.moveaxis(values[..., 1024:].reshape(2, n, 64, 6), 0, 2)
    return jnp.concatenate([main, tail], axis=-1).reshape(n, FF)


def pick(values, core):
    return lax.dynamic_index_in_dim(values, core, 0, keepdims=False)


def spread(offset):
    src = lax.broadcasted_iota(jnp.int32, (512, 1024), 0)
    dst = lax.broadcasted_iota(jnp.int32, (512, 1024), 1)
    return (dst == src // HEAD * 128 + src % HEAD + offset).astype(BF16)


def to_heads(values):
    n = values.shape[-1] // 8
    return values.reshape(2, 128, 8, n).transpose(0, 2, 1, 3).reshape(2048, n)


def from_heads(values):
    n = values.shape[-1]
    return values.reshape(2, 8, 128, n).transpose(0, 2, 1, 3).reshape(256, 8 * n)


def exchange(values):
    return lax.all_to_all(values, ("yl", "x", "yh"), 0, 0, tiled=True)


def dot(a, b):
    return jnp.dot(a, b, preferred_element_type=F32)


def body(
    tokens, cotangent, w_attn, w_ffn_in, w_down, gains, m_attn, m_ffn_in, m_down, m_gains,
    v_attn, v_ffn_in, v_down, v_gains,
):
    core = lax.axis_index("core")
    attn_low = w_attn.astype(BF16)
    ffn_low = w_ffn_in.astype(BF16)
    down_low = w_down.astype(BF16)
    qkv_low = attn_low[:3].reshape(3, 8, 2, 8, HEAD)
    key_value = jnp.stack([qkv_low[1], qkv_low[2]], axis=3)
    early = jnp.concatenate(
        [
            qkv_low[0].transpose(1, 0, 2, 3).reshape(2, 8, 512),
            key_value.transpose(1, 0, 2, 3, 4).reshape(2, 8, 1024),
        ],
        axis=-1,
    )
    late = jnp.concatenate([by_core(ffn_low[0]), by_core(ffn_low[1])], axis=-1)
    packed = jnp.concatenate([early, late], axis=-1)
    mine = pick(packed, core)
    theirs = other_core(pick(packed, 1 - core))
    rows16 = jnp.concatenate(
        [jnp.where(core == 0, mine, theirs), jnp.where(core == 0, theirs, mine)], axis=0
    )
    out_gain = jnp.concatenate(
        [
            attn_low[3],
            jnp.pad(gains.astype(BF16).T, ((0, 0), (0, 126))),
        ],
        axis=-1,
    )
    out_gain = both(core, out_gain, 0)
    shard_one = jnp.concatenate([rows16[:, :1536], out_gain[:, 1024:]], axis=-1)
    shard_two = jnp.concatenate(
        [rows16[:, 1536:], out_gain[:, :1024], down_low[:16], down_low[16:].reshape(16, 384)],
        axis=-1,
    )
    full_one = gather_chips(shard_one, 1, "gather_early")
    full_two = gather_chips(shard_two, 2, "gather_late")
    w_q = full_one[:, :512]
    w_kv = full_one[:, 512:1536]
    gain_one = full_one[:, 1536].astype(F32)
    gain_two = full_one[:, 1537].astype(F32)
    w_gate = full_two[:, :HALF]
    w_up = full_two[:, HALF : 2 * HALF]
    w_out = full_two[:, 2 * HALF : 2 * HALF + 1024]
    w_dn = jnp.concatenate(
        [
            full_two[:, 2 * HALF + 1024 : 2 * HALF + 2048],
            full_two[:, 2 * HALF + 2048 :].reshape(384, 1024),
        ],
        axis=0,
    )
    inputs = both(core, tokens, 1).astype(F32).reshape(256, WIDTH)
    grad_rows = both(core, cotangent, 1).reshape(256, WIDTH)

    scaled_one, inverse_one = normalize(inputs)
    normed_one = (scaled_one * gain_one).astype(BF16)
    queries = dot(dot(normed_one, w_q).astype(BF16), spread(0)).astype(BF16)
    keys_values = dot(normed_one, w_kv).astype(BF16)
    qkv = exchange(jnp.concatenate([to_heads(queries), to_heads(keys_values)], axis=-1))
    kv_all, att = attend(qkv, 3)
    att = from_heads(exchange(att))
    att_half = lax.dot_general(
        att, spread(HEAD), (((1,), (1,)), ((), ())), preferred_element_type=F32
    ).astype(BF16)
    attn_out = both(core, att_half, 1)
    middle = inputs + dot(attn_out, w_out)
    scaled_two, inverse_two = normalize(middle)
    normed_two = (scaled_two * gain_two).astype(BF16)
    gate = dot(normed_two, w_gate)
    upward = dot(normed_two, w_up)
    hidden = (jax.nn.silu(gate) * upward).astype(BF16)
    result_part = dot(hidden, w_dn).reshape(2, 2, 64, WIDTH)
    mid_own = pick(middle.reshape(2, 2, 64, WIDTH).swapaxes(0, 1), core)
    part_own = pick(result_part.swapaxes(0, 1), core)
    part_other = other_core(pick(result_part.swapaxes(0, 1), 1 - core))
    output = (mid_own + (part_own + part_other)).astype(BF16)

    grad_dn = outer_sum(hidden, grad_rows)
    grad_hidden = dot_nt(grad_rows, w_dn)
    squash = jax.nn.sigmoid(gate)
    grad_up = (grad_hidden * jax.nn.silu(gate)).astype(BF16)
    grad_gate = (grad_hidden * upward * (squash + gate * squash * (1.0 - squash))).astype(BF16)
    grad_normed_two = dot_nt(grad_gate, w_gate) + dot_nt(grad_up, w_up)
    grad_normed_two = grad_normed_two + other_core(grad_normed_two)
    gain_grad_two = jnp.sum(grad_normed_two * scaled_two, axis=0)
    grad_middle = grad_rows.astype(F32) + norm_back(
        grad_normed_two * gain_two, scaled_two, inverse_two
    )
    branch_grad = grad_middle.astype(BF16)
    w_out_half = lax.dynamic_slice_in_dim(w_out, core * 512, 512, 0)
    grad_att = dot_nt(branch_grad, w_out_half).astype(BF16)
    grad_att = exchange(to_heads(dot(grad_att, spread(HEAD)).astype(BF16)))
    grad_qkv = exchange(attend_back(qkv, kv_all, grad_att, 4))
    grad_q = lax.dot_general(
        from_heads(grad_qkv[:, :128]),
        spread(0),
        (((1,), (1,)), ((), ())),
        preferred_element_type=F32,
    ).astype(BF16)
    grad_kv = from_heads(grad_qkv[:, 128:])
    grad_normed_one = dot_nt(grad_q, w_q) + dot_nt(grad_kv, w_kv)
    grad_normed_one = grad_normed_one + other_core(grad_normed_one)
    gain_grad_one = jnp.sum(grad_normed_one * scaled_one, axis=0)
    grad_inputs = grad_middle + norm_back(grad_normed_one * gain_one, scaled_one, inverse_one)
    grad_inputs = pick(grad_inputs.reshape(2, 2, 64, WIDTH).swapaxes(0, 1), core)

    branch_half = lax.dynamic_slice_in_dim(branch_grad, core * 512, 512, 1)
    lanes = lax.broadcasted_iota(jnp.int32, (1024, 128), 1)
    gain_cols = jnp.where(lanes == 0, gain_grad_one[:, None], gain_grad_two[:, None])
    grads_two = jnp.concatenate(
        [
            outer_sum(normed_two, grad_gate).astype(BF16),
            outer_sum(normed_two, grad_up).astype(BF16),
            outer_sum(attn_out, branch_half).astype(BF16),
            grad_dn[:1024].astype(BF16),
            grad_dn[1024:].astype(BF16).reshape(1024, 384),
        ],
        axis=-1,
    )
    grads_one = jnp.concatenate(
        [
            outer_sum(normed_one, grad_q).astype(BF16),
            outer_sum(normed_one, grad_kv).astype(BF16),
            gain_cols.astype(BF16),
        ],
        axis=-1,
    )
    sum_two = scatter_chips(grads_two, 5, "scatter_ffn")
    sum_one = scatter_chips(grads_one, 6, "scatter_attn")

    wide = 2 * HALF + 512
    rows = jnp.concatenate([sum_two[:, :wide], sum_one[:, :1536]], axis=-1).reshape(2, 8, wide + 1536)
    mine = pick(rows, core)
    theirs = other_core(pick(rows, 1 - core))
    pair = jnp.stack([jnp.where(core == 0, mine, theirs), jnp.where(core == 0, theirs, mine)])
    ffn_part = jnp.stack([from_cores(pair[..., :HALF]), from_cores(pair[..., HALF : 2 * HALF])])
    out_part = jnp.concatenate([pair[0, :, 2 * HALF : wide], pair[1, :, 2 * HALF : wide]], axis=-1)
    q_part = pair[..., wide : wide + 512].transpose(1, 0, 2).reshape(8, 1024)
    kv_part = pair[..., wide + 512 :].reshape(2, 8, 8, 2, HEAD).transpose(3, 1, 0, 2, 4).reshape(2, 8, 1024)
    attn_part = jnp.concatenate([q_part[None], kv_part, out_part[None]], axis=0)
    down_part = jnp.concatenate(
        [sum_two[:, wide : wide + 1024], sum_two[:, wide + 1024 :].reshape(6, 1024)], axis=0
    )
    gain_part = pick(sum_one[:, 1536:1538].reshape(2, 8, 2), core).T

    new_attn, second_attn = adam_step(w_attn, m_attn, v_attn, attn_part, 0.06, 0.1)
    new_ffn, second_ffn = adam_step(w_ffn_in, m_ffn_in, v_ffn_in, ffn_part, 0.06, 0.1)
    new_dn, second_dn = adam_step(w_down, m_down, v_down, down_part, 0.04, 0.1)
    new_gn, second_gn = adam_step(gains, m_gains, v_gains, gain_part, 0.4, 0.0)
    return (
        output, grad_inputs, attn_part, ffn_part, down_part, gain_part,
        new_attn, new_ffn, new_dn, new_gn, second_attn, second_ffn, second_dn, second_gn,
    )


def solution(mesh):
    fine = Mesh(mesh.devices.reshape(2, 4, 4, 2, 2), AXES)
    rows3 = P(None, AXES, None)
    rows2 = P(AXES, None)
    cols = P(None, AXES)
    weights = (rows3, rows3, rows2, cols)
    return jax.shard_map(
        body,
        mesh=fine,
        in_specs=(rows3, rows3) + weights * 3,
        out_specs=(rows3, rows3) + weights * 3,
        check_vma=False,
    )
```

time: 2970 us -> 438 us (0.15)
  waiting for transfers between devices: 849 us -> 10.8 us
  local copies, waits for them, and re-layouts: 853 us -> 50.2 us
  blocking collectives: 645 us -> 0 us
  matrix products: 511 us -> 38.5 us
  Pallas kernels: 0 us -> 253 us
    dynamic_slice x144 -> x1, local copies, waits for them, and re-layouts: 818 us -> 0.01 us  [pick(): return lax.dynamic_index_in_dim(values, core, 0, keepdims=False)]
    all_gather x7 -> x0, waiting for transfers between devices: 679 us -> none  [the longest x1 238 us: body(): lax.all_gather(key_rows, ('blk', 'fsdp'), axis=1, tiled=True)]
    unnamed x2 -> x0, blocking collectives: 466 us -> none
    dot_general x110 -> x14, matrix products: 491 us -> 28.3 us  [the longest x7 16.8 us: dot(): return jnp.dot(a, b, preferred_element_type=F32)]
    pallas_call x0 -> x6, Pallas kernels: none -> 253 us  [the longest x2 86.7 us: gather_chips(): pl.pallas_call(gather_kernel, out_shape=jax.ShapeDtypeStruct((2, 4, 4, 2)...]
    all_gather x1 -> x0, blocking collectives: 179 us -> none  [body(): lax.all_gather(gains.astype(jnp.bfloat16), ('blk', 'fsdp'), axis=1, tiled...]
    reduce_scatter x2 -> x0, waiting for transfers between devices: 170 us -> none  [the longest x1 170 us: body(): lax.psum_scatter(attn_grad, ('blk', 'fsdp'), scatter_dimension=1, tiled=T...]
    ppermute x0 -> x9, starting transfers between devices: none -> 36.2 us  [other_core(): return lax.ppermute(values, 'core', SWAP)]
  transfers between devices with their start and end apart: 20 -> 13, of which waited for: 5 -> 5; matrix products, arithmetic and copies ran while one was open for 60% -> 13% of each run, Pallas kernels for 0% -> 52%
where the time goes in v1:
time: 438 us; the launch traced here: 431 us
  Pallas kernels  253 us (58%)
  starting transfers between devices  52.9 us (12%)
  local copies, waits for them, and re-layouts  50.2 us (11%)
  matrix products  38.5 us (9%)
  other arithmetic  22.7 us (5%)
  waiting for transfers between devices  10.8 us (2%)
    pallas_call x2, Pallas kernels, gather_chips(): pl.pallas_call(gather_kernel, out_shape=jax.ShapeDtypeStruct((2, 4, 4, 2)...  86.7 us
    pallas_call x2, Pallas kernels, scatter_chips(): pl.pallas_call(scatter_kernel, out_shape=jax.ShapeDtypeStruct((16, width)...  82.5 us
    pallas_call x1, Pallas kernels, attend_back(): pl.pallas_call(attend_back_kernel, out_shape=jax.ShapeDtypeStruct((n, 256...  50.1 us
    ppermute x9, starting transfers between devices, other_core(): return lax.ppermute(values, 'core', SWAP)  36.2 us
    pallas_call x1, Pallas kernels, attend(): pl.pallas_call(attend_kernel, out_shape=(jax.ShapeDtypeStruct((4, n, 128)...  33.8 us
    dot_general x7, matrix products, dot(): return jnp.dot(a, b, preferred_element_type=F32)  16.8 us
    all_to_all x4, starting transfers between devices, exchange(): return lax.all_to_all(values, ('yl', 'x', 'yh'), 0, 0, tiled=True)  16.8 us
    unnamed x148, local copies, waits for them, and re-layouts  16.3 us
  transfers between devices with their start and end apart: 13, of which 5 were waited for; matrix products, arithmetic and copies ran while one was open for 13% of the time, Pallas kernels for 52%

profile of v1, /device:TPU:1, one launch (start us, length us, event | category | flops | bytes accessed | tf_op | source)
XLA Modules:
  0.0 430.8 jit_solution(2373776538645015688)
XLA Ops:
  0.6 1.5 collective-permute-start
  11.8 31.8 %gather_early.1 = bf16[2,4,4,2,16,1664]{5,4,3,2,1,0:T(8,128)(2,1)} custom-call(bf16[16,1664]{1,0:T(8,128)(2,1)} %fusion.64.shard), custom_call_target="tpu_custom_call" | custom-call | tf_op jit(solution)/shard_map/gather_early/pallas_call | solution.py:134
  45.5 2.5 fusion.21
  48.3 2.2 fusion.24
  51.9 3.7 all-to-all-start
  55.5 7.0 %collective-permute-start.5 = (bf16[2,64,1024]{2,1,0:T(8,128)(2,1)S(1)}, bf16[2,64,1024]{2,1,0:T(8,128)(2,1)S(1)}, u32[]{:S(2)}, u32[]{:S(2)}) collective-permute-start(bf16[2,64,1024]{2,1,0:T(8,128)(2,1)S(1)} %copy-done.37), channel_id=1, source_target_pairs={{0,1},{1,0},{2,3},{3,2},{4,5},{5,4},{6,7},{7,6},{8,9},{9,8},{10,11... | collective-permute-start | bytes 786440 | tf_op jit(solution)/shard_map/ppermute | solution.py:511
  63.3 54.9 %gather_late.1 = bf16[2,4,4,2,16,5248]{5,4,3,2,1,0:T(8,128)(2,1)} custom-call(bf16[16,5248]{1,0:T(8,128)(2,1)} %fusion.51.shard), custom_call_target="tpu_custom_call" | custom-call | tf_op jit(solution)/shard_map/gather_late/pallas_call | solution.py:134
  119.6 1.8 reshape.281
  121.4 33.8 %attend.1 = (bf16[4,2048,128]{2,1,0:T(8,128)(2,1)S(1)}, bf16[2048,128]{1,0:T(8,128)(2,1)}) custom-call(bf16[2048,256]{1,0:T(8,128)(2,1)S(1)} %bitcast.184), custom_call_target="tpu_custom_call" | custom-call | tf_op jit(solution)/shard_map/attend/pallas_call | solution.py:372
  155.2 1.3 copy-done
  156.5 4.9 %all-to-all-start.1 = ((bf16[16,128,128]{2,1,0:T(8,128)(2,1)}), bf16[16,128,128]{2,1,0:T(8,128)(2,1)S(1)}, u32[]{:S(2)}, u32[]{:S(2)}) async-start(bf16[16,128,128]{2,1,0:T(8,128)(2,1)} %bitcast.19), calls=%async_computation.1 | async-start | bytes 1048576 | tf_op jit(solution)/shard_map/all_to_all | solution.py:556
  161.4 4.7 %fusion.93 = (bf16[1024,1024]{1,0:T(8,128)(2,1)}, bf16[1024,1024]{1,0:T(8,128)(2,1)}) fusion(bf16[1024,5248]{1,0:T(8,128)(2,1)} %bitcast.188), kind=kLoop, calls=%fused_computation.200 | loop fusion | bytes 8388608 | tf_op jit(solution)/shard_map/slice | solution.py:608
  166.2 4.2 all-to-all-done.1
  171.6 11.7 %collective-permute-start.3 = (bf16[256,512]{1,0:T(8,128)(2,1)S(1)}, bf16[256,512]{1,0:T(8,128)(2,1)S(1)}, u32[]{:S(2)}, u32[]{:S(2)}) collective-permute-start(bf16[256,512]{1,0:T(8,128)(2,1)S(1)} %convolution_convert_fusion.11), channel_id=1, source_target_pairs={{0,1},{1,0},{2,3},{3,2},{4,5},{5,4},{6,7},{7,6},{8,9},{9,8},{10,11... | collective-permute-start | bytes 786440 | tf_op jit(solution)/shard_map/ppermute | solution.py:511
  184.6 2.8 multiply_reduce_fusion.4
  187.6 3.0 fusion.2
  192.4 2.3 multiply_convert_fusion.1
  195.8 2.0 fusion.15
  199.6 3.8 convolution_convert_fusion.2
  203.4 2.6 convolution_convert_fusion.1
  206.0 2.0 multiply_reduce_fusion
  208.1 3.1 fusion.92
  211.2 2.4 fusion.25
  214.7 3.6 all-to-all-start.2
  218.3 3.0 fusion.10
  223.4 1.9 constant_dynamic-update-slice_fusion.10
  225.3 4.1 all-to-all-done.2
  229.4 1.6 copy-done.1
  231.0 50.1 %attend_back.1 = bf16[2048,256]{1,0:T(8,128)(2,1)} custom-call(bf16[2048,256]{1,0:T(8,128)(2,1)S(1)} %bitcast.185, bf16[4,2048,128]{2,1,0:T(8,128)(2,1)S(1)} %copy-done.1, bf16[2048,128]{1,0:T(8,128)(2,1)S(1)} %bitcast.186), custom_call_target="tpu_custom_call" | custom-call | tf_op jit(solution)/shard_map/attend_back/pallas_call | solution.py:464
  281.0 4.6 %all-to-all-start.3 = ((bf16[16,128,256]{2,1,0:T(8,128)(2,1)}), bf16[16,128,256]{2,1,0:T(8,128)(2,1)}, u32[]{:S(2)}, u32[]{:S(2)}) async-start(bf16[16,128,256]{2,1,0:T(8,128)(2,1)} %bitcast.33), calls=%async_computation.3 | async-start | bytes 2097152 | tf_op jit(solution)/shard_map/all_to_all | solution.py:556
  285.6 2.2 convolution_convert_fusion
  287.8 1.6 copy-done.2
  290.3 2.0 concatenate.90
  292.4 3.8 constant_dynamic-update-slice_fusion.9
  296.2 1.8 fusion.40
  300.5 1.3 fusion.94
  302.1 2.5 fusion.11
  305.9 1.8 convolution_add_fusion
  307.8 4.0 collective-permute-start.7
  311.8 1.5 constant_dynamic-update-slice_fusion.7
  314.4 54.3 %scatter_ffn.1 = f32[16,4736]{1,0:T(8,128)} custom-call(bf16[2,4,4,2,16,4736]{5,4,3,2,1,0:T(8,128)(2,1)} %constant_dynamic-update-slice_fusion.6.grads), custom_call_target="tpu_custom_call" | custom-call | tf_op jit(solution)/shard_map/scatter_ffn/pallas_call | solution.py:276
  368.7 1.3 slice.181
  370.0 1.5 slice.180
  372.2 1.8 multiply_subtract_fusion.2
  376.9 3.7 copy.145
  380.6 28.2 %scatter_attn.1 = f32[16,1664]{1,0:T(8,128)} custom-call(bf16[2,4,4,2,16,1664]{5,4,3,2,1,0:T(8,128)(2,1)} %bitcast.199), custom_call_target="tpu_custom_call" | custom-call | tf_op jit(solution)/shard_map/scatter_attn/pallas_call | solution.py:276
  410.5 10.6 %collective-permute-start.8 = (f32[8,4864]{1,0:T(8,128)S(1)}, f32[8,4864]{1,0:T(8,128)S(1)}, u32[]{:S(2)}, u32[]{:S(2)}) collective-permute-start(f32[8,4864]{1,0:T(8,128)S(1)} %dynamic-slice_bitcast_fusion.2), channel_id=1, source_target_pairs={{0,1},{1,0},{2,3},{3,2},{4,5},{5,4},{6,7},{7,6},{8,9},{9,8},{10,11... | collective-permute-start | bytes 466952 | tf_op jit(solution)/shard_map/ppermute | solution.py:511
  421.3 1.5 multiply_add_fusion
  (274 shorter events, 44.1 us)
Async XLA Ops:
  0.6 44.4 %collective-permute-start = (bf16[2,64,1024]{2,1,0:T(8,128)(2,1)}, bf16[2,64,1024]{2,1,0:T(8,128)(2,1)S(1)}, u32[]{:S(2)}, u32[]{:S(2)}) collective-permute-start(bf16[2,64,1024]{2,1,0:T(8,128)(2,1)} %param.14), channel_id=1, source_target_pairs={{0,1},{1,0},{2,3},{3,2},{4,5},{5,4},{6,7},{7,6},{8,9},{9,8},{10,11... | collective-permute-start | bytes 786440 | tf_op jit(solution)/shard_map/ppermute | solution.py:511
  3.9 6.4 %collective-permute-start.2 = (bf16[8,1152]{1,0:T(8,128)(2,1)S(1)}, bf16[8,1152]{1,0:T(8,128)(2,1)S(1)}, u32[]{:S(2)}, u32[]{:S(2)}) collective-permute-start(bf16[8,1152]{1,0:T(8,128)(2,1)S(1)} %fusion.68), channel_id=1, source_target_pairs={{0,1},{1,0},{2,3},{3,2},{4,5},{5,4},{6,7},{7,6},{8,9},{9,8},{10,11... | collective-permute-start | bytes 55304 | tf_op jit(solution)/shard_map/ppermute | solution.py:511
  9.7 1.5 collective-permute-start.1
  10.2 160.4 %copy-start.47 = (s32[512]{0:T(512)}, s32[512]{0:T(512)S(1)}, u32[]{:S(2)}) copy-start(s32[512]{0:T(512)S(1)} %get-tuple-element.73) | copy-start | bytes 6148
  10.2 38.0 %copy-start.49 = (s32[512]{0:T(512)}, s32[512]{0:T(512)S(1)}, u32[]{:S(2)}) copy-start(s32[512]{0:T(512)S(1)} %get-tuple-element.74) | copy-start | bytes 6148
  10.2 38.0 %copy-start.51 = (s32[512]{0:T(512)}, s32[512]{0:T(512)S(1)}, u32[]{:S(2)}) copy-start(s32[512]{0:T(512)S(1)} %get-tuple-element.75) | copy-start | bytes 6148
  10.3 38.0 %copy-start.57 = (pred[512]{0:T(512)(128)(4,1)}, pred[512]{0:T(512)(128)(4,1)S(1)}, u32[]{:S(2)}) copy-start(pred[512]{0:T(512)(128)(4,1)S(1)} %get-tuple-element.70) | copy-start | bytes 1540
  10.3 38.0 %copy-start.60 = (pred[512]{0:T(512)(128)(4,1)}, pred[512]{0:T(512)(128)(4,1)S(1)}, u32[]{:S(2)}) copy-start(pred[512]{0:T(512)(128)(4,1)S(1)} %get-tuple-element.71) | copy-start | bytes 1540
  11.8 33.2 %copy-start.36 = (bf16[2,64,1024]{2,1,0:T(8,128)(2,1)S(1)}, bf16[2,64,1024]{2,1,0:T(8,128)(2,1)}, u32[]{:S(2)}) copy-start(bf16[2,64,1024]{2,1,0:T(8,128)(2,1)} %param.14) | copy-start | bytes 786436
  45.1 330.2 %copy-start.4 = (bf16[2,64,1024]{2,1,0:T(8,128)(2,1)}, bf16[2,64,1024]{2,1,0:T(8,128)(2,1)S(1)}, u32[]{:S(2)}) copy-start(bf16[2,64,1024]{2,1,0:T(8,128)(2,1)S(1)} %get-tuple-element.47) | copy-start | bytes 786436
  45.1 330.2 %copy-start.6 = (bf16[2,64,1024]{2,1,0:T(8,128)(2,1)}, bf16[2,64,1024]{2,1,0:T(8,128)(2,1)S(1)}, u32[]{:S(2)}) copy-start(bf16[2,64,1024]{2,1,0:T(8,128)(2,1)S(1)} %get-tuple-element.48) | copy-start | bytes 786436
  50.7 4.8 %copy-start.37 = (bf16[2,64,1024]{2,1,0:T(8,128)(2,1)S(1)}, bf16[2,64,1024]{2,1,0:T(8,128)(2,1)}, u32[]{:S(2)}) copy-start(bf16[2,64,1024]{2,1,0:T(8,128)(2,1)} %param.15) | copy-start | bytes 786436
  50.7 11.8 %copy-start.35 = (f32[22,1024]{1,0:T(8,128)S(1)}, f32[22,1024]{1,0:T(8,128)}, u32[]{:S(2)}) copy-start(f32[22,1024]{1,0:T(8,128)} %param.18) | copy-start | bytes 270340
  51.9 69.5 %all-to-all-start = ((bf16[16,128,256]{2,1,0:T(8,128)(2,1)}), bf16[16,128,256]{2,1,0:T(8,128)(2,1)S(1)}, u32[]{:S(2)}, u32[]{:S(2)}) async-start(bf16[16,128,256]{2,1,0:T(8,128)(2,1)} %pad_maximum_fusion.4), calls=%async_computation | async-start | bytes 2097152 | tf_op jit(solution)/shard_map/all_to_all | solution.py:556
  55.5 110.6 %collective-permute-start.5 = (bf16[2,64,1024]{2,1,0:T(8,128)(2,1)S(1)}, bf16[2,64,1024]{2,1,0:T(8,128)(2,1)S(1)}, u32[]{:S(2)}, u32[]{:S(2)}) collective-permute-start(bf16[2,64,1024]{2,1,0:T(8,128)(2,1)S(1)} %copy-done.37), channel_id=1, source_target_pairs={{0,1},{1,0},{2,3},{3,2},{4,5},{5,4},{6,7},{7,6},{8,9},{9,8},{10,11... | collective-permute-start | bytes 786440 | tf_op jit(solution)/shard_map/ppermute | solution.py:511
  156.5 13.8 %all-to-all-start.1 = ((bf16[16,128,128]{2,1,0:T(8,128)(2,1)}), bf16[16,128,128]{2,1,0:T(8,128)(2,1)S(1)}, u32[]{:S(2)}, u32[]{:S(2)}) async-start(bf16[16,128,128]{2,1,0:T(8,128)(2,1)} %bitcast.19), calls=%async_computation.1 | async-start | bytes 1048576 | tf_op jit(solution)/shard_map/all_to_all | solution.py:556
  166.1 4.6 %copy-start.50 = (s32[512]{0:T(512)S(1)}, s32[512]{0:T(512)}, u32[]{:S(2)}) copy-start(s32[512]{0:T(512)} %copy-done.49) | copy-start | bytes 6148
  166.1 4.6 %copy-start.52 = (s32[512]{0:T(512)S(1)}, s32[512]{0:T(512)}, u32[]{:S(2)}) copy-start(s32[512]{0:T(512)} %copy-done.51) | copy-start | bytes 6148
  166.1 4.6 %copy-start.58 = (pred[512]{0:T(512)(128)(4,1)S(1)}, pred[512]{0:T(512)(128)(4,1)}, u32[]{:S(2)}) copy-start(pred[512]{0:T(512)(128)(4,1)} %copy-done.57) | copy-start | bytes 1540
  166.1 4.6 %copy-start.61 = (pred[512]{0:T(512)(128)(4,1)S(1)}, pred[512]{0:T(512)(128)(4,1)}, u32[]{:S(2)}) copy-start(pred[512]{0:T(512)(128)(4,1)} %copy-done.60) | copy-start | bytes 1540
  170.3 20.3 %slice-start = ((s8[10747904]{0:T(1024)(128)(4,1)}), s8[4194304]{0:T(1024)(128)(4,1)S(1)}, s32[]{:S(2)}) async-start(s8[10747904]{0:T(1024)(128)(4,1)} %bitcast.191), calls=%async_computation.4 | async-start | bytes 8388608
  171.6 12.9 %collective-permute-start.3 = (bf16[256,512]{1,0:T(8,128)(2,1)S(1)}, bf16[256,512]{1,0:T(8,128)(2,1)S(1)}, u32[]{:S(2)}, u32[]{:S(2)}) collective-permute-start(bf16[256,512]{1,0:T(8,128)(2,1)S(1)} %convolution_convert_fusion.11), channel_id=1, source_target_pairs={{0,1},{1,0},{2,3},{3,2},{4,5},{5,4},{6,7},{7,6},{8,9},{9,8},{10,11... | collective-permute-start | bytes 786440 | tf_op jit(solution)/shard_map/ppermute | solution.py:511
  183.3 7.3 %slice-start.1 = ((s8[10747904]{0:T(1024)(128)(4,1)}), s8[4194304]{0:T(1024)(128)(4,1)S(1)}, s32[]{:S(2)}) async-start(s8[10747904]{0:T(1024)(128)(4,1)} %bitcast.191), calls=%async_computation.5 | async-start | bytes 8388608
  183.4 8.3 %copy-start.12 = (bf16[2,128,1024]{2,1,0:T(8,128)(2,1)}, bf16[2,128,1024]{2,1,0:T(8,128)(2,1)S(1)}, u32[]{:S(2)}) copy-start(bf16[2,128,1024]{2,1,0:T(8,128)(2,1)S(1)} %pad_maximum_fusion.7) | copy-start | bytes 1572868
  184.6 6.1 %slice-start.2 = ((s8[10747904]{0:T(1024)(128)(4,1)}), s8[2359296]{0:T(1024)(128)(4,1)S(1)}, s32[]{:S(2)}) async-start(s8[10747904]{0:T(1024)(128)(4,1)} %bitcast.191), calls=%async_computation.6 | async-start | bytes 4718592
  187.4 20.6 %copy-start.8 = (f32[256,1024]{1,0:T(8,128)}, f32[256,1024]{1,0:T(8,128)S(1)}, u32[]{:S(2)}) copy-start(f32[256,1024]{1,0:T(8,128)S(1)} %get-tuple-element.69) | copy-start | bytes 3145732
  197.8 8.3 %collective-permute-start.6 = (f32[256,1024]{1,0:T(8,128)}, f32[256,1024]{1,0:T(8,128)}, u32[]{:S(2)}, u32[]{:S(2)}) collective-permute-start(f32[256,1024]{1,0:T(8,128)} %fusion.15), channel_id=1, source_target_pairs={{0,1},{1,0},{2,3},{3,2},{4,5},{5,4},{6,7},{7,6},{8,9},{9,8},{10,11... | collective-permute-start | bytes 3145736 | tf_op jit(solution)/shard_map/ppermute | solution.py:511
  213.6 4.7 %copy-start.16 = (bf16[256,1408]{1,0:T(8,128)(2,1)S(1)}, bf16[256,1408]{1,0:T(8,128)(2,1)}, u32[]{:S(2)}) copy-start(bf16[256,1408]{1,0:T(8,128)(2,1)} %get-tuple-element.39) | copy-start | bytes 2162692
  214.7 14.7 %all-to-all-start.2 = ((bf16[16,128,128]{2,1,0:T(8,128)(2,1)}), bf16[16,128,128]{2,1,0:T(8,128)(2,1)S(1)}, u32[]{:S(2)}, u32[]{:S(2)}) async-start(bf16[16,128,128]{2,1,0:T(8,128)(2,1)} %bitcast.31), calls=%async_computation.2 | async-start | bytes 1048576 | tf_op jit(solution)/shard_map/all_to_all | solution.py:556
  218.2 5.1 %copy-start.3 = (bf16[1024,1408]{1,0:T(8,128)(2,1)S(1)}, bf16[1024,1408]{1,0:T(8,128)(2,1)}, u32[]{:S(2)}) copy-start(bf16[1024,1408]{1,0:T(8,128)(2,1)} %convolution_convert_fusion.2) | copy-start | bytes 8650756
  223.0 73.2 %collective-permute-start.4 = (f32[2,64,1024]{2,1,0:T(8,128)}, f32[2,64,1024]{2,1,0:T(8,128)}, u32[]{:S(2)}, u32[]{:S(2)}) collective-permute-start(f32[2,64,1024]{2,1,0:T(8,128)} %dynamic-slice_bitcast_fusion.1), channel_id=1, source_target_pairs={{0,1},{1,0},{2,3},{3,2},{4,5},{5,4},{6,7},{7,6},{8,9},{9,8},{10,11... | collective-permute-start | bytes 1572872 | tf_op jit(solution)/shard_map/ppermute | solution.py:511
  281.0 19.4 %all-to-all-start.3 = ((bf16[16,128,256]{2,1,0:T(8,128)(2,1)}), bf16[16,128,256]{2,1,0:T(8,128)(2,1)}, u32[]{:S(2)}, u32[]{:S(2)}) async-start(bf16[16,128,256]{2,1,0:T(8,128)(2,1)} %bitcast.33), calls=%async_computation.3 | async-start | bytes 2097152 | tf_op jit(solution)/shard_map/all_to_all | solution.py:556
  292.4 3.9 copy-start.9
  292.4 3.9 copy-start.24
  292.4 5.7 %copy-start.33 = (bf16[256,1024]{1,0:T(8,128)(2,1)S(1)}, bf16[256,1024]{1,0:T(8,128)(2,1)}, u32[]{:S(2)}) copy-start(bf16[256,1024]{1,0:T(8,128)(2,1)} %get-tuple-element.32) | copy-start | bytes 1572868
  292.4 5.7 %copy-start.39 = (bf16[256,512]{1,0:T(8,128)(2,1)S(1)}, bf16[256,512]{1,0:T(8,128)(2,1)}, u32[]{:S(2)}) copy-start(bf16[256,512]{1,0:T(8,128)(2,1)} %copy-done.38) | copy-start | bytes 786436
  292.4 5.7 %copy-start.41 = (bf16[256,512]{1,0:T(8,128)(2,1)S(1)}, bf16[256,512]{1,0:T(8,128)(2,1)}, u32[]{:S(2)}) copy-start(bf16[256,512]{1,0:T(8,128)(2,1)} %copy-done.40) | copy-start | bytes 786436
  305.9 5.9 %slice-start.3 = ((bf16[1408,1024]{1,0:T(8,128)(2,1)}), bf16[1024,1024]{1,0:T(8,128)(2,1)S(1)}, s32[]{:S(2)}) async-start(bf16[1408,1024]{1,0:T(8,128)(2,1)} %copy-done.2), calls=%async_computation.7 | async-start | bytes 4194304 | tf_op jit(solution)/shard_map/slice | solution.py:679
  307.8 67.5 %copy-start.10 = (f32[256,1024]{1,0:T(8,128)}, f32[256,1024]{1,0:T(8,128)S(1)}, u32[]{:S(2)}) copy-start(f32[256,1024]{1,0:T(8,128)S(1)} %convolution_add_fusion) | copy-start | bytes 3145732
  307.8 67.5 %collective-permute-start.7 = (f32[256,1024]{1,0:T(8,128)S(1)}, f32[256,1024]{1,0:T(8,128)S(1)}, u32[]{:S(2)}, u32[]{:S(2)}) collective-permute-start(f32[256,1024]{1,0:T(8,128)S(1)} %convolution_add_fusion), channel_id=1, source_target_pairs={{0,1},{1,0},{2,3},{3,2},{4,5},{5,4},{6,7},{7,6},{8,9},{9,8},{10,11... | collective-permute-start | bytes 3145736 | tf_op jit(solution)/shard_map/ppermute | solution.py:511
  314.4 59.6 %copy-start.18 = (bf16[256,1024]{1,0:T(8,128)(2,1)S(1)}, bf16[256,1024]{1,0:T(8,128)(2,1)}, u32[]{:S(2)}) copy-start(bf16[256,1024]{1,0:T(8,128)(2,1)} %copy-done.17) | copy-start | bytes 1572868
  314.4 59.6 %copy-start.26 = (bf16[256,512]{1,0:T(8,128)(2,1)S(1)}, bf16[256,512]{1,0:T(8,128)(2,1)}, u32[]{:S(2)}) copy-start(bf16[256,512]{1,0:T(8,128)(2,1)} %copy-done.25) | copy-start | bytes 786436
  380.6 29.9 %slice-start.4 = ((f32[16,4736]{1,0:T(8,128)}), f32[16,3328]{1,0:T(8,128)S(1)}, s32[]{:S(2)}) async-start(f32[16,4736]{1,0:T(8,128)} %scatter_ffn.1), calls=%async_computation.8 | async-start | bytes 425984 | tf_op jit(solution)/shard_map/slice | solution.py:696
  380.6 40.7 %copy-start.5 = (bf16[2,64,1024]{2,1,0:T(8,128)(2,1)S(1)}, bf16[2,64,1024]{2,1,0:T(8,128)(2,1)}, u32[]{:S(2)}) copy-start(bf16[2,64,1024]{2,1,0:T(8,128)(2,1)} %copy-done.4) | copy-start | bytes 786436
  380.6 40.7 %copy-start.7 = (bf16[2,64,1024]{2,1,0:T(8,128)(2,1)S(1)}, bf16[2,64,1024]{2,1,0:T(8,128)(2,1)}, u32[]{:S(2)}) copy-start(bf16[2,64,1024]{2,1,0:T(8,128)(2,1)} %copy-done.6) | copy-start | bytes 786436
  380.6 40.7 %copy-start.11 = (f32[256,1024]{1,0:T(8,128)S(1)}, f32[256,1024]{1,0:T(8,128)}, u32[]{:S(2)}) copy-start(f32[256,1024]{1,0:T(8,128)} %copy-done.10) | copy-start | bytes 3145732
  380.6 40.7 %copy-start.15 = (f32[256,1024]{1,0:T(8,128)S(1)}, f32[256,1024]{1,0:T(8,128)}, u32[]{:S(2)}) copy-start(f32[256,1024]{1,0:T(8,128)} %copy-done.14) | copy-start | bytes 3145732
  410.5 13.8 %collective-permute-start.8 = (f32[8,4864]{1,0:T(8,128)S(1)}, f32[8,4864]{1,0:T(8,128)S(1)}, u32[]{:S(2)}, u32[]{:S(2)}) collective-permute-start(f32[8,4864]{1,0:T(8,128)S(1)} %dynamic-slice_bitcast_fusion.2), channel_id=1, source_target_pairs={{0,1},{1,0},{2,3},{3,2},{4,5},{5,4},{6,7},{7,6},{8,9},{9,8},{10,11... | collective-permute-start | bytes 466952 | tf_op jit(solution)/shard_map/ppermute | solution.py:511
  (33 other events, 64.9 us)
